TPU v7x, 128 devices: a whole 4x4x4 slice. The times are simulated.
128 devices in a mesh: row: 16 (over y, z), col: 8 (over x, core).
Axes of the slice: x: 4, y: 4, z: 4, core: 2. Of those that a mesh axis runs over, the one named last changes fastest.
Arguments:
- tokens: bfloat16 [256, 12288], P('row', 'col'), may hold values from -6 to 6
- out_grad: bfloat16 [256, 12288], P('row', 'col'), may hold values from -2 to 2
- w1_blocks: bfloat16 [23040, 128, 128], P(('row', 'col')), may hold values from -0.078125 to 0.078125
- w1_index: int32 [23040, 2], P(('row', 'col')), may hold values from 0 to 24, as said below
- w2_blocks: bfloat16 [23040, 128, 128], P(('row', 'col')), may hold values from -0.0390625 to 0.0390625
- w2_index: int32 [23040, 2], P(('row', 'col')), may hold values from 0 to 23, as said below
Outputs:
- output: bfloat16 [256, 12288], P('row', 'col')
- grad_input: bfloat16 [256, 12288], P('row', 'col')
- grad_w1: bfloat16 [23040, 128, 128], P(('row', 'col'))
- grad_w2: bfloat16 [23040, 128, 128], P(('row', 'col'))
Inputs may be any that keep to these rules, and one draw needn't show every extreme that they name: `w1_index`: within each tile's 180 slots the filled ones name distinct blocks of the tile; a slot with column 24 is empty and its row is any block row; in every draw some tile fills all 180 slots and some tile fills 180 // 2 of them. `w2_index`: within each tile's 180 slots the filled ones name distinct blocks of the tile; a slot with column 12 is empty and its row is any block row; in every draw some tile fills all 180 slots and some tile fills 180 // 2 of them.
All inputs are finite; a program needn't handle non-finite values.
Results may differ from a plain program's by a relative error of at most 0.03.
Values may be sent and summed in bfloat16 or wider, within the bound.
A program may use at most 256 MiB of HBM per device.

v0:
```python
import jax
import jax.numpy as jnp
from jax import lax
from jax.experimental import pallas as pl
from jax.experimental.pallas import tpu as pltpu
from jax.sharding import PartitionSpec as P

MESH = pl.DeviceIdType.MESH
BLK = 128
CAP = 180
FB = 12
UB = 24
FT = FB * BLK
UT = UB * BLK
TOK = 256
ITEMS = 4
NU = UT // ITEMS
UPI = UB // ITEMS
PER = UPI * FB
F32 = jnp.float32
BF16 = jnp.bfloat16
I32 = jnp.int32
NT = (((1,), (1,)), ((), ()))

ORDER = (
    "F0h F0g F1h 10h", "F1g 10g 11h F2h", "11g 20h F2g 12h", "20g F3h 21h 12g",
    "F3g 21g 13h 30h", "22h 30g 13g 31h", "22g 31g T0h 23h", "40h 50h 32h 40g",
    "50g 23g 51h 41h", "32g 51g 41g 33h", "52h 60h 60g 42h", "33g B0h 42g 61h",
    "B0g 43h 61g 52g", "53h B1h 43g 62h", "B1g 62g 63h 53g", "B2h 63g B2g B3h",
    "C0h B3g C0g W0h", "W0g C1h C1g W1h", "C2h C2g W1g C3h", "C3g W2h C4h C4g",
    "W2g W3h W3g C5h", "C5g",
)


def gelu_pair(value):
    cubic_term = 0.044715 * value * value * value
    tangent = jnp.tanh(0.7978845608 * (value + cubic_term))
    result = 0.5 * value * (1.0 + tangent)
    derivative = 0.5 * (1.0 + tangent) + 0.5 * value * (1.0 - tangent * tangent) * 0.7978845608 * (
        1.0 + 3.0 * 0.044715 * value * value
    )
    return (result, derivative)


def add(a, b):
    return (a.astype(F32) + b.astype(F32)).astype(BF16)


def fused_kernel(
    tok_ref,
    grad_ref,
    idx1_ref,
    idx2_ref,
    w1_hbm,
    w2_hbm,
    out_ref,
    gin_ref,
    dw1_hbm,
    dw2_hbm,
    w1v,
    w2v,
    dense1,
    dense2,
    full,
    part,
    rc,
    m1a,
    m1b,
    m2,
    slope,
    ag,
    acc,
    po,
    c1,
    c2,
    tok_t,
    act_t,
    inv_v,
    inv_s,
    send_sems,
    recv_sems,
    local_sems,
):
    row = lax.axis_index("row")
    col = lax.axis_index("col")
    y, z = row // 4, row % 4
    x, k = col // 2, col % 2
    yr, yl, yo = (y + 1) % 4, (y + 3) % 4, (y + 2) % 4
    zr, zl, zo = (z + 1) % 4, (z + 3) % 4, (z + 2) % 4
    xr, xl, xo = (x + 1) % 4, (x + 3) % 4, (x + 2) % 4
    sib = (row, x * 2 + 1 - k)
    dev_xr, dev_xl = (row, xr * 2 + k), (row, xl * 2 + k)
    dev_y = tuple((p * 4 + z, col) for p in (yr, yl, yo))
    dev_z = tuple((y * 4 + p, col) for p in (zr, zl, zo))

    load1 = pltpu.make_async_copy(w1_hbm, w1v.at[pl.ds(0, CAP)], local_sems.at[0])
    load2 = pltpu.make_async_copy(w2_hbm, w2v.at[pl.ds(0, CAP)], local_sems.at[1])
    load1.start()
    load2.start()

    barrier = pltpu.get_barrier_semaphore()
    for dev in (sib, dev_xr, dev_xl) + dev_y + dev_z:
        pl.semaphore_signal(barrier, inc=1, device_id=dev, device_id_type=MESH)

    full[0, y, z] = tok_ref[...]
    full[1, y, z] = grad_ref[...]
    w1v[CAP] = jnp.zeros((BLK, BLK), BF16)
    w2v[CAP] = jnp.zeros((BLK, BLK), BF16)
    inv_v[...] = jnp.full((8, BLK), CAP, I32)
    for n, (idx, width) in enumerate(((idx1_ref, UB), (idx2_ref, FB))):
        i, j = idx[0:1, :], idx[1:2, :]
        target = jnp.where(j < width, i * width + j, 511)
        spread = jnp.broadcast_to(target, (BLK, CAP)).T
        slots = lax.broadcasted_iota(I32, (CAP, BLK), 0)
        places = lax.broadcasted_iota(I32, (CAP, BLK), 1)
        for m in range(3):
            found = jnp.where(spread == places + m * BLK, slots, CAP)
            inv_v[n * 3 + m : n * 3 + m + 1, :] = jnp.min(found, axis=0, keepdims=True)
    table = pltpu.make_async_copy(inv_v, inv_s, local_sems.at[2])
    table.start()
    pl.semaphore_wait(barrier, 9)

    started = []

    def send(src, dst, dev):
        n = len(started)
        copy = pltpu.make_async_remote_copy(
            src_ref=src,
            dst_ref=dst,
            send_sem=send_sems.at[n],
            recv_sem=recv_sems.at[n],
            device_id=dev,
            device_id_type=MESH,
        )
        copy.start()
        started.append(copy)
        return copy

    def slot(a, p, q):
        return full.at[a, q, p] if a == 0 else full.at[a, p, q]

    near = ((z, zr, zl, zo), (y, yr, yl, yo))
    own = (y, z)
    first = (dev_z, dev_y)
    second = (dev_y, dev_z)

    def spread_to(ref, devs):
        return [send(ref, ref, dev) for dev in devs]

    stage_a = [spread_to(slot(a, near[a][0], own[a]), first[a]) for a in (0, 1)]
    stage_b = [[spread_to(slot(a, near[a][0], own[a]), second[a])] for a in (0, 1)]

    def fill1(i, carry):
        for j in range(UB):
            p = i * UB + j
            dense1[pl.ds(pl.multiple_of(i * BLK, BLK), BLK), pl.ds(j * BLK, BLK)] = w1v[inv_s[p >> 7, p & 127]]
        return carry

    def fill2(i, carry):
        for j in range(FB):
            p = i * FB + j
            dense2[pl.ds(pl.multiple_of(i * BLK, BLK), BLK), pl.ds(j * BLK, BLK)] = w2v[inv_s[3 + (p >> 7), p & 127]]
        return carry

    table.wait()
    load1.wait()
    lax.fori_loop(0, FB, fill1, 0)
    for step, mirror in ((1, 1), (2, 0), (3, 2)):
        for a in (0, 1):
            stage_a[a][mirror].wait_recv()
            stage_b[a].append(spread_to(slot(a, near[a][step], own[a]), second[a]))
        if step == 2:
            load2.wait()
            lax.fori_loop(0, UB, fill2, 0)
    for a in (0, 1):
        for copies in stage_b[a]:
            for copy in copies:
                copy.wait_recv()

    ahead = (dev_xr, dev_xl)
    behind = (dev_xl, dev_xr)
    x_ahead = (xr, xl)
    x_behind = (xl, xr)
    flight = {}

    def step_f(u, a):
        tokens = full[a].reshape(TOK, FT)
        if a == 0:
            hidden = jnp.dot(tokens, dense1[:, pl.ds(u * NU, NU)], preferred_element_type=F32)
        else:
            hidden = lax.dot_general(tokens, dense2[pl.ds(u * NU, NU), :], NT, preferred_element_type=F32)
        part[a, u] = hidden.astype(BF16).reshape(2, 4, 32, NU)
        flight["core", u, a] = send(part.at[a, u, 1 - k], rc.at[a, u], sib)

    def step_1(u, a):
        flight["core", u, a].wait_recv()
        for where in (xo, x_behind[a], x_ahead[a], x):
            part[a, u, k, where] = add(part[a, u, k, where], rc[a, u, where])
        flight["m1a", u, a] = send(part.at[a, u, k, xo], m1a.at[a, u], ahead[a])
        flight["m1b", u, a] = send(part.at[a, u, k, x_behind[a]], m1b.at[a, u], behind[a])

    def step_2(u, a):
        flight["m1a", u, a].wait_recv()
        part[a, u, k, x_ahead[a]] = add(part[a, u, k, x_ahead[a]], m1a[a, u])
        flight["m2", u, a] = send(part.at[a, u, k, x_ahead[a]], m2.at[a, u], ahead[a])

    def step_3(u, a):
        flight["m1b", u, a].wait_recv()
        flight["m2", u, a].wait_recv()
        total = part[a, u, k, x].astype(F32) + m1b[a, u].astype(F32) + m2[a, u].astype(F32)
        if a == 0:
            act, rate = gelu_pair(total)
            slope[u] = rate
            ag[a, u, k, x] = act.astype(BF16)
        else:
            ag[a, u, k, x] = (total * slope[u]).astype(BF16)
        mine = ag.at[a, u, k, x]
        flight["agd", u, a] = send(mine, mine, ahead[a])
        flight["ago", u, a] = send(mine, mine, behind[a])
        flight["s0", u, a] = send(mine, mine, sib)

    def step_4(u, a):
        flight["agd", u, a].wait_recv()
        got = ag.at[a, u, k, x_behind[a]]
        flight["fwd", u, a] = send(got, got, ahead[a])
        flight["s1", u, a] = send(got, got, sib)

    def step_5(u, a):
        flight["ago", u, a].wait_recv()
        got = ag.at[a, u, k, x_ahead[a]]
        flight["s2", u, a] = send(got, got, sib)

    def step_6(u, a):
        flight["fwd", u, a].wait_recv()
        got = ag.at[a, u, k, xo]
        flight["s3", u, a] = send(got, got, sib)

    def step_b(u, a):
        for name in ("s0", "s1", "s2", "s3"):
            flight[name, u, a].wait_recv()
        base = pl.ds(u * NU, NU)
        width = FT // 2
        for n in range(2):
            here = pl.ds(n * width, width)
            units = ag[a, u].reshape(TOK, NU)
            if a == 0:
                value = jnp.dot(units, dense2[base, here], preferred_element_type=F32)
            else:
                value = lax.dot_general(units, dense1[here, base], NT, preferred_element_type=F32)
            if u > 0:
                value = value + acc[a, :, here]
            if u < ITEMS - 1:
                acc[a, :, here] = value
            else:
                po[a, :, :, :, here] = value.astype(BF16).reshape(4, 4, 16, width)

    def step_t(u, a):
        for i in range(FB):
            tok_t[pl.ds(i * BLK, BLK), :] = full[0, :, :, :, pl.ds(i * BLK, BLK)].reshape(TOK, BLK).T

    saves = {}

    def step_w(u, a):
        stage, target = ((w2v, dw2_hbm), (w1v, dw1_hbm))[a]
        base = (u % 2) * PER
        if u >= 2:
            saves[u - 2, a].wait()
        if a == 1:
            for n in range(NU // 256):
                pre = ag[1, u, :, :, :, pl.ds(n * 256, 256)].reshape(TOK, 256)
                value = jnp.dot(tok_t[...], pre, preferred_element_type=F32).astype(BF16)
                for c in range(2):
                    piece = value[:, c * BLK : (c + 1) * BLK].reshape(FB, BLK, BLK)
                    stage[pl.ds(base + (2 * n + c) * FB, FB)] = piece
        else:
            for i in range(UPI):
                act_t[pl.ds(i * BLK, BLK), :] = ag[0, u, :, :, :, pl.ds(i * BLK, BLK)].reshape(TOK, BLK).T
            for n in range(FT // 256):
                grads = full[1, :, :, :, pl.ds(n * 256, 256)].reshape(TOK, 256)
                value = jnp.dot(act_t[...], grads, preferred_element_type=F32).astype(BF16)
                for c in range(2):
                    piece = value[:, c * BLK : (c + 1) * BLK].reshape(UPI, BLK, BLK)
                    stage[pl.ds(base + (2 * n + c) * UPI, UPI)] = piece
        save = pltpu.make_async_copy(
            stage.at[pl.ds(base, PER)], target.at[pl.ds(u * PER, PER)], local_sems.at[3 + 2 * u + a]
        )
        save.start()
        saves[u, a] = save

    def piece(a, p, q):
        return po.at[a, p, q] if a == 0 else po.at[a, q, p]

    far = ((zo, zr, zl, z), (yo, yr, yl, y))
    mine_p = (y, z)
    peers = ((yr, yl, yo), (zr, zl, zo))
    peer_devs = (dev_y, dev_z)
    last_devs = ((dev_z[2], dev_z[0], dev_z[1]), (dev_y[2], dev_y[0], dev_y[1]))

    def step_c(u, a):
        if u == 0:
            for n in range(4):
                flight["c1", n, a] = [
                    send(piece(a, peers[a][d], far[a][n]), c1.at[a, n, d], peer_devs[a][d]) for d in (2, 0, 1)
                ]
        elif u <= 4:
            n = u - 1
            for copy in flight["c1", n, a]:
                copy.wait_recv()
            spot = piece(a, mine_p[a], far[a][n])
            total = spot[...].astype(F32)
            for d in range(3):
                total = total + c1[a, n, d].astype(F32)
            spot[...] = total.astype(BF16)
            if n < 3:
                flight["c2", n, a] = send(spot, c2.at[a, n], last_devs[a][n])
        else:
            total = piece(a, mine_p[a], far[a][3])[...].astype(F32)
            for n in range(3):
                flight["c2", n, a].wait_recv()
                total = total + c2[a, n].astype(F32)
            (out_ref, gin_ref)[a][...] = total.astype(BF16)

    steps = {
        "F": step_f,
        "1": step_1,
        "2": step_2,
        "3": step_3,
        "4": step_4,
        "5": step_5,
        "6": step_6,
        "B": step_b,
        "T": step_t,
        "W": step_w,
        "C": step_c,
    }
    for line in ORDER:
        for name in line.split():
            steps[name[0]](int(name[1]), "hg".index(name[2]))

    for copy in started:
        copy.wait_send()
    for u in range(max(ITEMS - 2, 0), ITEMS):
        saves[u, 0].wait()
        saves[u, 1].wait()


N_SEMS = 30 + 22 * ITEMS + 30


def fused(tokens, out_grad, idx1, idx2, w1, w2):
    vmem = pl.BlockSpec(memory_space=pltpu.VMEM)
    hbm = pl.BlockSpec(memory_space=pl.ANY)
    flops = 6 * 2 * TOK * FT * UT
    return pl.pallas_call(
        fused_kernel,
        out_shape=(
            jax.ShapeDtypeStruct((16, FT), BF16),
            jax.ShapeDtypeStruct((16, FT), BF16),
            jax.ShapeDtypeStruct((FB * UB, BLK, BLK), BF16),
            jax.ShapeDtypeStruct((FB * UB, BLK, BLK), BF16),
        ),
        in_specs=[vmem, vmem, vmem, vmem, hbm, hbm],
        out_specs=(vmem, vmem, hbm, hbm),
        scratch_shapes=[
            pltpu.VMEM((CAP + 1, BLK, BLK), BF16),
            pltpu.VMEM((CAP + 1, BLK, BLK), BF16),
            pltpu.VMEM((FT, UT), BF16),
            pltpu.VMEM((UT, FT), BF16),
            pltpu.VMEM((2, 4, 4, 16, FT), BF16),
            pltpu.VMEM((2, ITEMS, 2, 4, 32, NU), BF16),
            pltpu.VMEM((2, ITEMS, 4, 32, NU), BF16),
            pltpu.VMEM((2, ITEMS, 32, NU), BF16),
            pltpu.VMEM((2, ITEMS, 32, NU), BF16),
            pltpu.VMEM((2, ITEMS, 32, NU), BF16),
            pltpu.VMEM((ITEMS, 32, NU), F32),
            pltpu.VMEM((2, ITEMS, 2, 4, 32, NU), BF16),
            pltpu.VMEM((2, TOK, FT), F32),
            pltpu.VMEM((2, 4, 4, 16, FT), BF16),
            pltpu.VMEM((2, 4, 3, 16, FT), BF16),
            pltpu.VMEM((2, 3, 16, FT), BF16),
            pltpu.VMEM((FT, TOK), BF16),
            pltpu.VMEM((NU, TOK), BF16),
            pltpu.VMEM((8, BLK), I32),
            pltpu.SMEM((8, BLK), I32),
            pltpu.SemaphoreType.DMA((N_SEMS,)),
            pltpu.SemaphoreType.DMA((N_SEMS,)),
            pltpu.SemaphoreType.DMA((3 + 2 * ITEMS,)),
        ],
        compiler_params=pltpu.CompilerParams(
            collective_id=0, has_side_effects=True, vmem_limit_bytes=60 * 1024 * 1024
        ),
        cost_estimate=pl.CostEstimate(flops=flops, bytes_accessed=31_000_000, transcendentals=200_000),
        name="ffn_fused",
    )(tokens, out_grad, idx1, idx2, w1, w2)


def place_kernel(
    idx1_ref, idx2_ref, dw1, dw2, out_in, gin_in, gw1, gw2, out, gin, zero, sem1, sem2, sem3
):
    zero[...] = jnp.zeros((BLK, BLK), BF16)
    outs = (pltpu.make_async_copy(out_in, out, sem3.at[0]), pltpu.make_async_copy(gin_in, gin, sem3.at[1]))
    for copy in outs:
        copy.start()

    def one(s, carry):
        i, j = idx1_ref[0, s], idx1_ref[1, s]
        kept = j < UB

        @pl.when(kept)
        def _():
            pltpu.make_async_copy(dw1.at[j * FB + i], gw1.at[s], sem1).start()

        @pl.when(jnp.logical_not(kept))
        def _():
            pltpu.make_async_copy(zero, gw1.at[s], sem1).start()

        i2, j2 = idx2_ref[0, s], idx2_ref[1, s]
        kept2 = j2 < FB

        @pl.when(kept2)
        def _():
            pltpu.make_async_copy(dw2.at[(i2 // UPI) * PER + j2 * UPI + i2 % UPI], gw2.at[s], sem2).start()

        @pl.when(jnp.logical_not(kept2))
        def _():
            pltpu.make_async_copy(zero, gw2.at[s], sem2).start()

        return carry

    lax.fori_loop(0, CAP, one, 0, unroll=4)
    pltpu.make_async_copy(dw1.at[pl.ds(0, CAP)], gw1, sem1).wait()
    pltpu.make_async_copy(dw2.at[pl.ds(0, CAP)], gw2, sem2).wait()
    for copy in outs:
        copy.wait()


def place(idx1, idx2, dw1, dw2, out, gin):
    smem = pl.BlockSpec(memory_space=pltpu.SMEM)
    hbm = pl.BlockSpec(memory_space=pl.ANY)
    shape = jax.ShapeDtypeStruct((CAP, BLK, BLK), BF16)
    small = jax.ShapeDtypeStruct((16, FT), BF16)
    return pl.pallas_call(
        place_kernel,
        out_shape=(shape, shape, small, small),
        in_specs=[smem, smem, hbm, hbm, hbm, hbm],
        out_specs=(hbm, hbm, hbm, hbm),
        scratch_shapes=[
            pltpu.VMEM((BLK, BLK), BF16),
            pltpu.SemaphoreType.DMA,
            pltpu.SemaphoreType.DMA,
            pltpu.SemaphoreType.DMA((2,)),
        ],
        cost_estimate=pl.CostEstimate(flops=0, bytes_accessed=24_000_000, transcendentals=0),
        name="ffn_place",
    )(idx1, idx2, dw1, dw2, out, gin)


def body(tokens, out_grad, w1_blocks, w1_index, w2_blocks, w2_index):
    idx1, idx2 = w1_index.T, w2_index.T
    output, grad_input, dw1, dw2 = fused(tokens, out_grad, idx1, idx2, w1_blocks, w2_blocks)
    grad_one, grad_two, output, grad_input = place(idx1, idx2, dw1, dw2, output, grad_input)
    return output, grad_input, grad_one, grad_two


def solution(mesh):
    return jax.shard_map(
        body,
        mesh=mesh,
        in_specs=(
            P("row", "col"),
            P("row", "col"),
            P(("row", "col"), None, None),
            P(("row", "col"), None),
            P(("row", "col"), None, None),
            P(("row", "col"), None),
        ),
        out_specs=(
            P("row", "col"),
            P("row", "col"),
            P(("row", "col"), None, None),
            P(("row", "col"), None, None),
        ),
        check_vma=False,
    )
```

profile of v0, /device:TPU:61, one launch (start us, length us, event | category | flops | bytes accessed | tf_op | source)
XLA Modules:
  0.0 428.7 jit_solution(4512416033112495211)
XLA Ops:
  0.6 68.6 %ffn_fused.1 = (bf16[16,1536]{1,0:T(8,128)(2,1)}, bf16[16,1536]{1,0:T(8,128)(2,1)}, bf16[288,128,128]{2,1,0:T(8,128)(2,1)}, bf16[288,128,128]{2,1,0:T(8,128)(2,1)}) custom-call(bf16[16,1536]{1,0:T(8,128)(2,1)} %tok_ref.1, bf16[16,1536]{1,0:T(8,128)(2,1)} %grad_ref.1, s32[2,180]{1,0:T(2,128)} %bitcast.2, s32[2,180]{1,0:T(2,128)} %bitcast.4, ...), custom_call_target="tpu_custom_call" | custom-call | flops 14495514624 | bytes 31000000 | tf_op jit(solution)/shard_map/ffn_fused/pallas_call | solution.py:354
  69.3 359.2 %ffn_place.1 = (bf16[180,128,128]{2,1,0:T(8,128)(2,1)}, bf16[180,128,128]{2,1,0:T(8,128)(2,1)}, bf16[16,1536]{1,0:T(8,128)(2,1)}, bf16[16,1536]{1,0:T(8,128)(2,1)}) custom-call(s32[2,180]{1,0:T(2,128)} %bitcast.3, s32[2,180]{1,0:T(2,128)} %bitcast.5, bf16[288,128,128]{2,1,0:T(8,128)(2,1)} %get-tuple-element.12.dw1, ...), custom_call_target="tpu_custom_call" | custom-call | bytes 24000000 | tf_op jit(solution)/shard_map/ffn_place/pallas_call | solution.py:442
where the time goes:
time: 429 us
  Pallas kernels  428 us (100%)
    pallas_call x1, Pallas kernels, place(): pl.pallas_call(place_kernel, out_shape=(shape, shape, small, small), in_s...  359 us
    pallas_call x1, Pallas kernels, fused(): pl.pallas_call(fused_kernel, out_shape=(jax.ShapeDtypeStruct((16, FT), BF...  68.6 us

commit v1 on v0

--- a/solution.py
+++ b/solution.py
@@ -20,6 +20,7 @@
 F32 = jnp.float32
 BF16 = jnp.bfloat16
 I32 = jnp.int32
+NONE = FB * UB
 NT = (((1,), (1,)), ((), ()))
 
 ORDER = (
@@ -27,8 +28,8 @@
     "F3g 21g 13h 30h", "22h 30g 13g 31h", "22g 31g T0h 23h", "40h 50h 32h 40g",
     "50g 23g 51h 41h", "32g 51g 41g 33h", "52h 60h 60g 42h", "33g B0h 42g 61h",
     "B0g 43h 61g 52g", "53h B1h 43g 62h", "B1g 62g 63h 53g", "B2h 63g B2g B3h",
-    "C0h B3g C0g W0h", "W0g C1h C1g W1h", "C2h C2g W1g C3h", "C3g W2h C4h C4g",
-    "W2g W3h W3g C5h", "C5g",
+    "C0h B3g C0g W0g", "W1g C1h C1g W2g", "C2h C2g W3g C3h", "C3g S0g C4h C4g",
+    "W0h W1h C5h C5g", "W2h W3h S0h",
 )
 
 
@@ -47,23 +48,21 @@
 
 
 def fused_kernel(
-    tok_ref,
-    grad_ref,
-    idx1_ref,
-    idx2_ref,
+    tok_hbm,
+    grad_hbm,
+    idx1_hbm,
+    idx2_hbm,
     w1_hbm,
     w2_hbm,
     out_ref,
     gin_ref,
     dw1_hbm,
     dw2_hbm,
-    w1v,
-    w2v,
+    wv,
     dense1,
     dense2,
     full,
     part,
-    rc,
     m1a,
     m1b,
     m2,
@@ -75,6 +74,9 @@
     c2,
     tok_t,
     act_t,
+    idx_v,
+    pos_v,
+    pos_s,
     inv_v,
     inv_s,
     send_sems,
@@ -93,23 +95,36 @@
     dev_y = tuple((p * 4 + z, col) for p in (yr, yl, yo))
     dev_z = tuple((y * 4 + p, col) for p in (zr, zl, zo))
 
-    load1 = pltpu.make_async_copy(w1_hbm, w1v.at[pl.ds(0, CAP)], local_sems.at[0])
-    load2 = pltpu.make_async_copy(w2_hbm, w2v.at[pl.ds(0, CAP)], local_sems.at[1])
+    load1 = pltpu.make_async_copy(w1_hbm, wv.at[pl.ds(0, CAP)], local_sems.at[0])
+    load2 = pltpu.make_async_copy(w2_hbm, wv.at[pl.ds(0, CAP)], local_sems.at[1])
+    loads = [
+        pltpu.make_async_copy(source, target, local_sems.at[3 + n])
+        for n, (source, target) in enumerate(
+            (
+                (idx1_hbm, idx_v.at[0]),
+                (idx2_hbm, idx_v.at[1]),
+                (tok_hbm, full.at[0, y, z]),
+                (grad_hbm, full.at[1, y, z]),
+            )
+        )
+    ]
+    for load in loads:
+        load.start()
     load1.start()
-    load2.start()
 
     barrier = pltpu.get_barrier_semaphore()
     for dev in (sib, dev_xr, dev_xl) + dev_y + dev_z:
         pl.semaphore_signal(barrier, inc=1, device_id=dev, device_id_type=MESH)
 
-    full[0, y, z] = tok_ref[...]
-    full[1, y, z] = grad_ref[...]
-    w1v[CAP] = jnp.zeros((BLK, BLK), BF16)
-    w2v[CAP] = jnp.zeros((BLK, BLK), BF16)
+    for ref, last in ((wv, CAP), (dense1, NONE), (dense2, NONE)):
+        ref[last] = jnp.zeros((BLK, BLK), BF16)
+    loads[0].wait()
+    loads[1].wait()
     inv_v[...] = jnp.full((8, BLK), CAP, I32)
-    for n, (idx, width) in enumerate(((idx1_ref, UB), (idx2_ref, FB))):
-        i, j = idx[0:1, :], idx[1:2, :]
-        target = jnp.where(j < width, i * width + j, 511)
+    for n, (height, width) in enumerate(((FB, UB), (UB, FB))):
+        i, j = idx_v[n, 0:1, :], idx_v[n, 1:2, :]
+        target = jnp.where(j < width, j * height + i, NONE)
+        pos_v[n : n + 1, :] = target
         spread = jnp.broadcast_to(target, (BLK, CAP)).T
         slots = lax.broadcasted_iota(I32, (CAP, BLK), 0)
         places = lax.broadcasted_iota(I32, (CAP, BLK), 1)
@@ -118,6 +133,10 @@
             inv_v[n * 3 + m : n * 3 + m + 1, :] = jnp.min(found, axis=0, keepdims=True)
     table = pltpu.make_async_copy(inv_v, inv_s, local_sems.at[2])
     table.start()
+    places_of = pltpu.make_async_copy(pos_v, pos_s, local_sems.at[7])
+    places_of.start()
+    for load in loads[2:]:
+        load.wait()
     pl.semaphore_wait(barrier, 9)
 
     started = []
@@ -150,28 +169,27 @@
     stage_a = [spread_to(slot(a, near[a][0], own[a]), first[a]) for a in (0, 1)]
     stage_b = [[spread_to(slot(a, near[a][0], own[a]), second[a])] for a in (0, 1)]
 
-    def fill1(i, carry):
-        for j in range(UB):
-            p = i * UB + j
-            dense1[pl.ds(pl.multiple_of(i * BLK, BLK), BLK), pl.ds(j * BLK, BLK)] = w1v[inv_s[p >> 7, p & 127]]
-        return carry
-
-    def fill2(i, carry):
-        for j in range(FB):
-            p = i * FB + j
-            dense2[pl.ds(pl.multiple_of(i * BLK, BLK), BLK), pl.ds(j * BLK, BLK)] = w2v[inv_s[3 + (p >> 7), p & 127]]
-        return carry
+    def fill(dense, first_row):
+        def some(m, carry):
+            for n in range(12):
+                p = m * 12 + n
+                dense[p] = wv[inv_s[first_row + (p >> 7), p & 127]]
+            return carry
+
+        lax.fori_loop(0, FB * UB // 12, some, 0)
 
     table.wait()
+    places_of.wait()
     load1.wait()
-    lax.fori_loop(0, FB, fill1, 0)
+    fill(dense1, 0)
+    load2.start()
     for step, mirror in ((1, 1), (2, 0), (3, 2)):
         for a in (0, 1):
             stage_a[a][mirror].wait_recv()
             stage_b[a].append(spread_to(slot(a, near[a][step], own[a]), second[a]))
         if step == 2:
             load2.wait()
-            lax.fori_loop(0, UB, fill2, 0)
+            fill(dense2, 3)
     for a in (0, 1):
         for copies in stage_b[a]:
             for copy in copies:
@@ -183,19 +201,29 @@
     x_behind = (xl, xr)
     flight = {}
 
+    def tile1(u, rows, count):
+        return jnp.concatenate(
+            [dense1[pl.ds(j * FB + rows, count)].reshape(count * BLK, BLK) for j in range(u * UPI, (u + 1) * UPI)], axis=1
+        )
+
+    def tile2(u, columns, count):
+        return jnp.concatenate(
+            [dense2[pl.ds(j * UB + u * UPI, UPI)].reshape(NU, BLK) for j in range(columns, columns + count)], axis=1
+        )
+
     def step_f(u, a):
         tokens = full[a].reshape(TOK, FT)
         if a == 0:
-            hidden = jnp.dot(tokens, dense1[:, pl.ds(u * NU, NU)], preferred_element_type=F32)
+            hidden = jnp.dot(tokens, tile1(u, 0, FB), preferred_element_type=F32)
         else:
-            hidden = lax.dot_general(tokens, dense2[pl.ds(u * NU, NU), :], NT, preferred_element_type=F32)
+            hidden = lax.dot_general(tokens, tile2(u, 0, FB), NT, preferred_element_type=F32)
         part[a, u] = hidden.astype(BF16).reshape(2, 4, 32, NU)
-        flight["core", u, a] = send(part.at[a, u, 1 - k], rc.at[a, u], sib)
+        flight["core", u, a] = send(part.at[a, u, 1 - k], ag.at[a, u, 1 - k], sib)
 
     def step_1(u, a):
         flight["core", u, a].wait_recv()
         for where in (xo, x_behind[a], x_ahead[a], x):
-            part[a, u, k, where] = add(part[a, u, k, where], rc[a, u, where])
+            part[a, u, k, where] = add(part[a, u, k, where], ag[a, u, k, where])
         flight["m1a", u, a] = send(part.at[a, u, k, xo], m1a.at[a, u], ahead[a])
         flight["m1b", u, a] = send(part.at[a, u, k, x_behind[a]], m1b.at[a, u], behind[a])
 
@@ -238,15 +266,15 @@
     def step_b(u, a):
         for name in ("s0", "s1", "s2", "s3"):
             flight[name, u, a].wait_recv()
-        base = pl.ds(u * NU, NU)
         width = FT // 2
+        half = FB // 2
         for n in range(2):
             here = pl.ds(n * width, width)
             units = ag[a, u].reshape(TOK, NU)
             if a == 0:
-                value = jnp.dot(units, dense2[base, here], preferred_element_type=F32)
+                value = jnp.dot(units, tile2(u, n * half, half), preferred_element_type=F32)
             else:
-                value = lax.dot_general(units, dense1[here, base], NT, preferred_element_type=F32)
+                value = lax.dot_general(units, tile1(u, n * half, half), NT, preferred_element_type=F32)
             if u > 0:
                 value = value + acc[a, :, here]
             if u < ITEMS - 1:
@@ -258,34 +286,36 @@
         for i in range(FB):
             tok_t[pl.ds(i * BLK, BLK), :] = full[0, :, :, :, pl.ds(i * BLK, BLK)].reshape(TOK, BLK).T
 
-    saves = {}
-
     def step_w(u, a):
-        stage, target = ((w2v, dw2_hbm), (w1v, dw1_hbm))[a]
-        base = (u % 2) * PER
-        if u >= 2:
-            saves[u - 2, a].wait()
         if a == 1:
-            for n in range(NU // 256):
-                pre = ag[1, u, :, :, :, pl.ds(n * 256, 256)].reshape(TOK, 256)
-                value = jnp.dot(tok_t[...], pre, preferred_element_type=F32).astype(BF16)
-                for c in range(2):
-                    piece = value[:, c * BLK : (c + 1) * BLK].reshape(FB, BLK, BLK)
-                    stage[pl.ds(base + (2 * n + c) * FB, FB)] = piece
+            pre = ag[1, u].reshape(TOK, NU)
+            value = jnp.dot(tok_t[...], pre, preferred_element_type=F32).astype(BF16)
+            for c in range(UPI):
+                dense1[pl.ds((u * UPI + c) * FB, FB)] = value[:, c * BLK : (c + 1) * BLK].reshape(FB, BLK, BLK)
         else:
             for i in range(UPI):
                 act_t[pl.ds(i * BLK, BLK), :] = ag[0, u, :, :, :, pl.ds(i * BLK, BLK)].reshape(TOK, BLK).T
-            for n in range(FT // 256):
-                grads = full[1, :, :, :, pl.ds(n * 256, 256)].reshape(TOK, 256)
-                value = jnp.dot(act_t[...], grads, preferred_element_type=F32).astype(BF16)
-                for c in range(2):
-                    piece = value[:, c * BLK : (c + 1) * BLK].reshape(UPI, BLK, BLK)
-                    stage[pl.ds(base + (2 * n + c) * UPI, UPI)] = piece
-        save = pltpu.make_async_copy(
-            stage.at[pl.ds(base, PER)], target.at[pl.ds(u * PER, PER)], local_sems.at[3 + 2 * u + a]
-        )
+            grads = full[1].reshape(TOK, FT)
+            value = jnp.dot(act_t[...], grads, preferred_element_type=F32).astype(BF16)
+            for c in range(FB):
+                dense2[pl.ds(c * UB + u * UPI, UPI)] = value[:, c * BLK : (c + 1) * BLK].reshape(UPI, BLK, BLK)
+
+    saves = []
+
+    def step_s(u, a):
+        dense, target = ((dense2, dw2_hbm), (dense1, dw1_hbm))[a]
+        for save in saves:
+            save.wait()
+
+        def some(m, carry):
+            for n in range(12):
+                wv[m * 12 + n] = dense[pos_s[1 - a, m * 12 + n]]
+            return carry
+
+        lax.fori_loop(0, CAP // 12, some, 0)
+        save = pltpu.make_async_copy(wv.at[pl.ds(0, CAP)], target, local_sems.at[9 + a])
         save.start()
-        saves[u, a] = save
+        saves.append(save)
 
     def piece(a, p, q):
         return po.at[a, p, q] if a == 0 else po.at[a, q, p]
@@ -331,6 +361,7 @@
         "B": step_b,
         "T": step_t,
         "W": step_w,
+        "S": step_s,
         "C": step_c,
     }
     for line in ORDER:
@@ -339,9 +370,7 @@
 
     for copy in started:
         copy.wait_send()
-    for u in range(max(ITEMS - 2, 0), ITEMS):
-        saves[u, 0].wait()
-        saves[u, 1].wait()
+    saves[-1].wait()
 
 
 N_SEMS = 30 + 22 * ITEMS + 30
@@ -356,19 +385,17 @@
         out_shape=(
             jax.ShapeDtypeStruct((16, FT), BF16),
             jax.ShapeDtypeStruct((16, FT), BF16),
-            jax.ShapeDtypeStruct((FB * UB, BLK, BLK), BF16),
-            jax.ShapeDtypeStruct((FB * UB, BLK, BLK), BF16),
+            jax.ShapeDtypeStruct((CAP, BLK, BLK), BF16),
+            jax.ShapeDtypeStruct((CAP, BLK, BLK), BF16),
         ),
-        in_specs=[vmem, vmem, vmem, vmem, hbm, hbm],
+        in_specs=[pl.BlockSpec(memory_space=pltpu.HBM)] * 6,
         out_specs=(vmem, vmem, hbm, hbm),
         scratch_shapes=[
             pltpu.VMEM((CAP + 1, BLK, BLK), BF16),
-            pltpu.VMEM((CAP + 1, BLK, BLK), BF16),
-            pltpu.VMEM((FT, UT), BF16),
-            pltpu.VMEM((UT, FT), BF16),
+            pltpu.VMEM((NONE + 1, BLK, BLK), BF16),
+            pltpu.VMEM((NONE + 1, BLK, BLK), BF16),
             pltpu.VMEM((2, 4, 4, 16, FT), BF16),
             pltpu.VMEM((2, ITEMS, 2, 4, 32, NU), BF16),
-            pltpu.VMEM((2, ITEMS, 4, 32, NU), BF16),
             pltpu.VMEM((2, ITEMS, 32, NU), BF16),
             pltpu.VMEM((2, ITEMS, 32, NU), BF16),
             pltpu.VMEM((2, ITEMS, 32, NU), BF16),
@@ -380,85 +407,57 @@
             pltpu.VMEM((2, 3, 16, FT), BF16),
             pltpu.VMEM((FT, TOK), BF16),
             pltpu.VMEM((NU, TOK), BF16),
+            pltpu.VMEM((2, 2, CAP), I32),
+            pltpu.VMEM((2, CAP), I32),
+            pltpu.SMEM((2, CAP), I32),
             pltpu.VMEM((8, BLK), I32),
             pltpu.SMEM((8, BLK), I32),
             pltpu.SemaphoreType.DMA((N_SEMS,)),
             pltpu.SemaphoreType.DMA((N_SEMS,)),
-            pltpu.SemaphoreType.DMA((3 + 2 * ITEMS,)),
+            pltpu.SemaphoreType.DMA((11,)),
         ],
         compiler_params=pltpu.CompilerParams(
-            collective_id=0, has_side_effects=True, vmem_limit_bytes=60 * 1024 * 1024
+            collective_id=0, has_side_effects=True, vmem_limit_bytes=42 * 1024 * 1024
         ),
         cost_estimate=pl.CostEstimate(flops=flops, bytes_accessed=31_000_000, transcendentals=200_000),
         name="ffn_fused",
     )(tokens, out_grad, idx1, idx2, w1, w2)
 
 
-def place_kernel(
-    idx1_ref, idx2_ref, dw1, dw2, out_in, gin_in, gw1, gw2, out, gin, zero, sem1, sem2, sem3
-):
-    zero[...] = jnp.zeros((BLK, BLK), BF16)
-    outs = (pltpu.make_async_copy(out_in, out, sem3.at[0]), pltpu.make_async_copy(gin_in, gin, sem3.at[1]))
-    for copy in outs:
+def place_kernel(dw1, dw2, out_in, gin_in, gw1, gw2, out, gin, sems):
+    copies = [
+        pltpu.make_async_copy(source, target, sems.at[n])
+        for n, (source, target) in enumerate(((dw1, gw1), (dw2, gw2), (out_in, out), (gin_in, gin)))
+    ]
+    for copy in copies:
         copy.start()
-
-    def one(s, carry):
-        i, j = idx1_ref[0, s], idx1_ref[1, s]
-        kept = j < UB
-
-        @pl.when(kept)
-        def _():
-            pltpu.make_async_copy(dw1.at[j * FB + i], gw1.at[s], sem1).start()
-
-        @pl.when(jnp.logical_not(kept))
-        def _():
-            pltpu.make_async_copy(zero, gw1.at[s], sem1).start()
-
-        i2, j2 = idx2_ref[0, s], idx2_ref[1, s]
-        kept2 = j2 < FB
-
-        @pl.when(kept2)
-        def _():
-            pltpu.make_async_copy(dw2.at[(i2 // UPI) * PER + j2 * UPI + i2 % UPI], gw2.at[s], sem2).start()
-
-        @pl.when(jnp.logical_not(kept2))
-        def _():
-            pltpu.make_async_copy(zero, gw2.at[s], sem2).start()
-
-        return carry
-
-    lax.fori_loop(0, CAP, one, 0, unroll=4)
-    pltpu.make_async_copy(dw1.at[pl.ds(0, CAP)], gw1, sem1).wait()
-    pltpu.make_async_copy(dw2.at[pl.ds(0, CAP)], gw2, sem2).wait()
-    for copy in outs:
+    for copy in copies:
         copy.wait()
 
 
-def place(idx1, idx2, dw1, dw2, out, gin):
-    smem = pl.BlockSpec(memory_space=pltpu.SMEM)
+def place(dw1, dw2, out, gin):
     hbm = pl.BlockSpec(memory_space=pl.ANY)
     shape = jax.ShapeDtypeStruct((CAP, BLK, BLK), BF16)
     small = jax.ShapeDtypeStruct((16, FT), BF16)
     return pl.pallas_call(
         place_kernel,
         out_shape=(shape, shape, small, small),
-        in_specs=[smem, smem, hbm, hbm, hbm, hbm],
+        in_specs=[hbm, hbm, hbm, hbm],
         out_specs=(hbm, hbm, hbm, hbm),
-        scratch_shapes=[
-            pltpu.VMEM((BLK, BLK), BF16),
-            pltpu.SemaphoreType.DMA,
-            pltpu.SemaphoreType.DMA,
-            pltpu.SemaphoreType.DMA((2,)),
-        ],
+        scratch_shapes=[pltpu.SemaphoreType.DMA((4,))],
+        compiler_params=pltpu.CompilerParams(vmem_limit_bytes=2 * 1024 * 1024),
         cost_estimate=pl.CostEstimate(flops=0, bytes_accessed=24_000_000, transcendentals=0),
         name="ffn_place",
-    )(idx1, idx2, dw1, dw2, out, gin)
+    )(dw1, dw2, out, gin)
 
 
 def body(tokens, out_grad, w1_blocks, w1_index, w2_blocks, w2_index):
     idx1, idx2 = w1_index.T, w2_index.T
+    tokens, out_grad, idx1, idx2 = [
+        pltpu.with_memory_space_constraint(value, pltpu.HBM) for value in (tokens, out_grad, idx1, idx2)
+    ]
     output, grad_input, dw1, dw2 = fused(tokens, out_grad, idx1, idx2, w1_blocks, w2_blocks)
-    grad_one, grad_two, output, grad_input = place(idx1, idx2, dw1, dw2, output, grad_input)
+    grad_one, grad_two, output, grad_input = place(dw1, dw2, output, grad_input)
     return output, grad_input, grad_one, grad_two
 
 

time: 429 us -> 77.7 us (0.18)
  the two profiles are of different devices: /device:TPU:61 before, /device:TPU:0 now
where the time goes in v1:
time: 77.7 us; the launch traced here: 77.6 us
  Pallas kernels  76.8 us (99%)
  between operations  0.8 us (1%)
    pallas_call x1, Pallas kernels, fused(): pl.pallas_call(fused_kernel, out_shape=(jax.ShapeDtypeStruct((16, FT), BF...  72.2 us
    pallas_call x1, Pallas kernels, place(): pl.pallas_call(place_kernel, out_shape=(shape, shape, small, small), in_s...  4.56 us

profile of v1, /device:TPU:0, one launch (start us, length us, event | category | flops | bytes accessed | tf_op | source)
XLA Modules:
  0.0 77.6 jit_solution(17535416730652637151)
XLA Ops:
  0.6 72.2 %ffn_fused.1 = (bf16[16,1536]{1,0:T(8,128)(2,1)S(1)}, bf16[16,1536]{1,0:T(8,128)(2,1)S(1)}, bf16[180,128,128]{2,1,0:T(8,128)(2,1)S(1)}, bf16[180,128,128]{2,1,0:T(8,128)(2,1)S(1)}) custom-call(bf16[16,1536]{1,0:T(8,128)(2,1)} %tok_hbm.1, bf16[16,1536]{1,0:T(8,128)(2,1)} %grad_hbm.1, s32[2,180]{1,0:T(2,128)} %bitcast.2, s32[2,180]{1,0:T(2,128)} %bitcast.3, ...), custom_call_target="tpu_custom_call" | custom-call | flops 14495514624 | bytes 31000000 | tf_op jit(solution)/shard_map/ffn_fused/pallas_call | solution.py:383
  72.9 4.6 %ffn_place.1 = (bf16[180,128,128]{2,1,0:T(8,128)(2,1)}, bf16[180,128,128]{2,1,0:T(8,128)(2,1)}, bf16[16,1536]{1,0:T(8,128)(2,1)}, bf16[16,1536]{1,0:T(8,128)(2,1)}) custom-call(bf16[180,128,128]{2,1,0:T(8,128)(2,1)S(1)} %get-tuple-element.12.dw1, bf16[180,128,128]{2,1,0:T(8,128)(2,1)S(1)} %get-tuple-element.13.dw2, ...), custom_call_target="tpu_custom_call" | custom-call | bytes 24000000 | tf_op jit(solution)/shard_map/ffn_place/pallas_call | solution.py:442

commit v2 on v1

--- a/solution.py
+++ b/solution.py
@@ -13,7 +13,7 @@
 FT = FB * BLK
 UT = UB * BLK
 TOK = 256
-ITEMS = 4
+ITEMS = 6
 NU = UT // ITEMS
 UPI = UB // ITEMS
 PER = UPI * FB
@@ -24,12 +24,14 @@
 NT = (((1,), (1,)), ((), ()))
 
 ORDER = (
-    "F0h F0g F1h 10h", "F1g 10g 11h F2h", "11g 20h F2g 12h", "20g F3h 21h 12g",
-    "F3g 21g 13h 30h", "22h 30g 13g 31h", "22g 31g T0h 23h", "40h 50h 32h 40g",
-    "50g 23g 51h 41h", "32g 51g 41g 33h", "52h 60h 60g 42h", "33g B0h 42g 61h",
-    "B0g 43h 61g 52g", "53h B1h 43g 62h", "B1g 62g 63h 53g", "B2h 63g B2g B3h",
-    "C0h B3g C0g W0g", "W1g C1h C1g W2g", "C2h C2g W3g C3h", "C3g S0g C4h C4g",
-    "W0h W1h C5h C5g", "W2h W3h S0h",
+    "F0h F1h F2h F3h", "10h 11h F4h 12h", "F5h 13h F0g 14h", "F1g 20h 15h 21h",
+    "F2g 10g 22h F3g", "11g 23h F4g 12g", "24h 30h 13g 25h", "T0h 31h 14g 20g",
+    "32h 21g 33h 22g", "F5g 50h 34h 40h", "15g 23g 35h 51h", "41h 24g 42h 30g",
+    "31g 52h 53h 43h", "44h 32g 60h 54h", "25g B0h 45h 33g", "55h 61h W0h 62h",
+    "34g B1h 40g 50g", "B2h 41g 51g 64h", "63h W1h 52g 42g", "W2h B3h 65h 35g",
+    "43g 53g B4h 44g", "54g B5h 60g 61g", "C0h 62g 45g 55g", "B0g 63g 64g B1g",
+    "B2g B3g B4g C1h", "65g W3h C2h W4h", "B5g C0g C3h C4h", "W5h S0h W0g W1g",
+    "W2g C1g W3g W4g", "C2g W5g S0g C3g", "C4g C5h C5g",
 )
 
 
@@ -64,8 +66,7 @@
     full,
     part,
     m1a,
-    m1b,
-    m2,
+    mm,
     slope,
     ag,
     acc,
@@ -103,8 +104,8 @@
             (
                 (idx1_hbm, idx_v.at[0]),
                 (idx2_hbm, idx_v.at[1]),
-                (tok_hbm, full.at[0, y, z]),
-                (grad_hbm, full.at[1, y, z]),
+                (tok_hbm, full.at[y * 4 + z]),
+                (grad_hbm, full.at[16 + y * 4 + z]),
             )
         )
     ]
@@ -115,6 +116,68 @@
     barrier = pltpu.get_barrier_semaphore()
     for dev in (sib, dev_xr, dev_xl) + dev_y + dev_z:
         pl.semaphore_signal(barrier, inc=1, device_id=dev, device_id_type=MESH)
+
+    for load in loads[2:]:
+        load.wait()
+    pl.semaphore_wait(barrier, 9)
+
+    used = [0]
+
+    def fresh():
+        used[0] += 1
+        return used[0] - 1
+
+    def send(src, dst, dev, group, recv=None):
+        copy = pltpu.make_async_remote_copy(
+            src_ref=src,
+            dst_ref=dst,
+            send_sem=send_sems.at[group],
+            recv_sem=recv_sems.at[fresh() if recv is None else recv],
+            device_id=dev,
+            device_id_type=MESH,
+        )
+        copy.start()
+        return copy
+
+    def wait_bytes(ref, sem):
+        pltpu.make_async_copy(ref, ref, sem).wait()
+
+    half = FT // 2
+    lanes = (pl.ds(0, half), pl.ds(half, half))
+
+    def slot(a, h, p, q):
+        spot = q * 4 + p if h == 0 else p * 4 + q
+        return full.at[a * 16 + spot, :, lanes[h]]
+
+    near = ((z, zr, zl, zo), (y, yr, yl, yo))
+    own = (y, z)
+    first = (dev_z, dev_y)
+    second = (dev_y, dev_z)
+
+    def spread_to(ref, devs, recv=None):
+        return [send(ref, ref, dev, 0, recv) for dev in devs]
+
+    def gather_one(a):
+        return [spread_to(slot(a, h, near[h][0], own[h]), first[h]) for h in (0, 1)]
+
+    everything = (fresh(), fresh())
+
+    def gather_two(a, step):
+        for h in (0, 1):
+            spread_to(slot(a, h, near[h][step], own[h]), second[h], everything[a])
+
+    def fill(dense, first_row):
+        def some(m, carry):
+            for n in range(12):
+                p = m * 12 + n
+                dense[p] = wv[inv_s[first_row + (p >> 7), p & 127]]
+            return carry
+
+        lax.fori_loop(0, FB * UB // 12, some, 0)
+
+    stage_a = [gather_one(0), None]
+    gather_two(0, 0)
+    stage_a[1] = gather_one(1)
 
     for ref, last in ((wv, CAP), (dense1, NONE), (dense2, NONE)):
         ref[last] = jnp.zeros((BLK, BLK), BF16)
@@ -135,65 +198,27 @@
     table.start()
     places_of = pltpu.make_async_copy(pos_v, pos_s, local_sems.at[7])
     places_of.start()
-    for load in loads[2:]:
-        load.wait()
-    pl.semaphore_wait(barrier, 9)
-
-    started = []
-
-    def send(src, dst, dev):
-        n = len(started)
-        copy = pltpu.make_async_remote_copy(
-            src_ref=src,
-            dst_ref=dst,
-            send_sem=send_sems.at[n],
-            recv_sem=recv_sems.at[n],
-            device_id=dev,
-            device_id_type=MESH,
-        )
-        copy.start()
-        started.append(copy)
-        return copy
-
-    def slot(a, p, q):
-        return full.at[a, q, p] if a == 0 else full.at[a, p, q]
-
-    near = ((z, zr, zl, zo), (y, yr, yl, yo))
-    own = (y, z)
-    first = (dev_z, dev_y)
-    second = (dev_y, dev_z)
-
-    def spread_to(ref, devs):
-        return [send(ref, ref, dev) for dev in devs]
-
-    stage_a = [spread_to(slot(a, near[a][0], own[a]), first[a]) for a in (0, 1)]
-    stage_b = [[spread_to(slot(a, near[a][0], own[a]), second[a])] for a in (0, 1)]
-
-    def fill(dense, first_row):
-        def some(m, carry):
-            for n in range(12):
-                p = m * 12 + n
-                dense[p] = wv[inv_s[first_row + (p >> 7), p & 127]]
-            return carry
-
-        lax.fori_loop(0, FB * UB // 12, some, 0)
-
+    def gather_rest(a):
+        for step, mirror in ((1, 1), (2, 0), (3, 2)):
+            for h in (0, 1):
+                stage_a[a][h][mirror].wait_recv()
+            gather_two(a, step)
+
+    gather_rest(0)
+    gather_two(1, 0)
     table.wait()
     places_of.wait()
     load1.wait()
     fill(dense1, 0)
     load2.start()
-    for step, mirror in ((1, 1), (2, 0), (3, 2)):
-        for a in (0, 1):
-            stage_a[a][mirror].wait_recv()
-            stage_b[a].append(spread_to(slot(a, near[a][step], own[a]), second[a]))
-        if step == 2:
-            load2.wait()
-            fill(dense2, 3)
-    for a in (0, 1):
-        for copies in stage_b[a]:
-            for copy in copies:
-                copy.wait_recv()
+    gather_rest(1)
+    load2.wait()
+    fill(dense2, 3)
+
+    def gathered(a):
+        wait_bytes(full.at[pl.ds(a * 16, 12)], recv_sems.at[everything[a]])
+
+    gathered(0)
 
     ahead = (dev_xr, dev_xl)
     behind = (dev_xl, dev_xr)
@@ -212,30 +237,35 @@
         )
 
     def step_f(u, a):
-        tokens = full[a].reshape(TOK, FT)
+        if a == 1 and u == 0:
+            gathered(1)
+        tokens = full[pl.ds(a * 16, 16)].reshape(TOK, FT)
         if a == 0:
             hidden = jnp.dot(tokens, tile1(u, 0, FB), preferred_element_type=F32)
         else:
             hidden = lax.dot_general(tokens, tile2(u, 0, FB), NT, preferred_element_type=F32)
         part[a, u] = hidden.astype(BF16).reshape(2, 4, 32, NU)
-        flight["core", u, a] = send(part.at[a, u, 1 - k], ag.at[a, u, 1 - k], sib)
+        flight["core", u, a] = send(part.at[a, u, 1 - k], ag.at[a, u, 1 - k], sib, 1)
 
     def step_1(u, a):
+        d = (u + a) % 2
         flight["core", u, a].wait_recv()
-        for where in (xo, x_behind[a], x_ahead[a], x):
+        for where in (xo, x_behind[d], x_ahead[d], x):
             part[a, u, k, where] = add(part[a, u, k, where], ag[a, u, k, where])
-        flight["m1a", u, a] = send(part.at[a, u, k, xo], m1a.at[a, u], ahead[a])
-        flight["m1b", u, a] = send(part.at[a, u, k, x_behind[a]], m1b.at[a, u], behind[a])
+        flight["m1a", u, a] = send(part.at[a, u, k, xo], m1a.at[a, u], ahead[d], 2)
+        flight["last", u, a] = fresh()
+        send(part.at[a, u, k, x_behind[d]], mm.at[a, u, 0], behind[d], 2, flight["last", u, a])
 
     def step_2(u, a):
+        d = (u + a) % 2
         flight["m1a", u, a].wait_recv()
-        part[a, u, k, x_ahead[a]] = add(part[a, u, k, x_ahead[a]], m1a[a, u])
-        flight["m2", u, a] = send(part.at[a, u, k, x_ahead[a]], m2.at[a, u], ahead[a])
+        part[a, u, k, x_ahead[d]] = add(part[a, u, k, x_ahead[d]], m1a[a, u])
+        send(part.at[a, u, k, x_ahead[d]], mm.at[a, u, 1], ahead[d], 2, flight["last", u, a])
 
     def step_3(u, a):
-        flight["m1b", u, a].wait_recv()
-        flight["m2", u, a].wait_recv()
-        total = part[a, u, k, x].astype(F32) + m1b[a, u].astype(F32) + m2[a, u].astype(F32)
+        d = (u + a) % 2
+        wait_bytes(mm.at[a, u], recv_sems.at[flight["last", u, a]])
+        total = part[a, u, k, x].astype(F32) + mm[a, u, 0].astype(F32) + mm[a, u, 1].astype(F32)
         if a == 0:
             act, rate = gelu_pair(total)
             slope[u] = rate
@@ -243,38 +273,42 @@
         else:
             ag[a, u, k, x] = (total * slope[u]).astype(BF16)
         mine = ag.at[a, u, k, x]
-        flight["agd", u, a] = send(mine, mine, ahead[a])
-        flight["ago", u, a] = send(mine, mine, behind[a])
-        flight["s0", u, a] = send(mine, mine, sib)
+        flight["agd", u, a] = send(mine, mine, ahead[d], 2)
+        flight["ago", u, a] = send(mine, mine, behind[d], 2)
+
+    arrived = {}
+
+    def count(u, a):
+        arrived[u, a] = arrived.get((u, a), 0) + 1
+        if arrived[u, a] == 3:
+            flight["s", u, a] = send(ag.at[a, u, k], ag.at[a, u, k], sib, 1)
 
     def step_4(u, a):
+        d = (u + a) % 2
         flight["agd", u, a].wait_recv()
-        got = ag.at[a, u, k, x_behind[a]]
-        flight["fwd", u, a] = send(got, got, ahead[a])
-        flight["s1", u, a] = send(got, got, sib)
+        got = ag.at[a, u, k, x_behind[d]]
+        flight["fwd", u, a] = send(got, got, ahead[d], 2)
+        count(u, a)
 
     def step_5(u, a):
         flight["ago", u, a].wait_recv()
-        got = ag.at[a, u, k, x_ahead[a]]
-        flight["s2", u, a] = send(got, got, sib)
+        count(u, a)
 
     def step_6(u, a):
         flight["fwd", u, a].wait_recv()
-        got = ag.at[a, u, k, xo]
-        flight["s3", u, a] = send(got, got, sib)
+        count(u, a)
 
     def step_b(u, a):
-        for name in ("s0", "s1", "s2", "s3"):
-            flight[name, u, a].wait_recv()
+        flight["s", u, a].wait_recv()
         width = FT // 2
-        half = FB // 2
+        rows = FB // 2
         for n in range(2):
             here = pl.ds(n * width, width)
             units = ag[a, u].reshape(TOK, NU)
             if a == 0:
-                value = jnp.dot(units, tile2(u, n * half, half), preferred_element_type=F32)
+                value = jnp.dot(units, tile2(u, n * rows, rows), preferred_element_type=F32)
             else:
-                value = lax.dot_general(units, tile1(u, n * half, half), NT, preferred_element_type=F32)
+                value = lax.dot_general(units, tile1(u, n * rows, rows), NT, preferred_element_type=F32)
             if u > 0:
                 value = value + acc[a, :, here]
             if u < ITEMS - 1:
@@ -284,7 +318,7 @@
 
     def step_t(u, a):
         for i in range(FB):
-            tok_t[pl.ds(i * BLK, BLK), :] = full[0, :, :, :, pl.ds(i * BLK, BLK)].reshape(TOK, BLK).T
+            tok_t[pl.ds(i * BLK, BLK), :] = full[pl.ds(0, 16), :, pl.ds(i * BLK, BLK)].reshape(TOK, BLK).T
 
     def step_w(u, a):
         if a == 1:
@@ -295,7 +329,7 @@
         else:
             for i in range(UPI):
                 act_t[pl.ds(i * BLK, BLK), :] = ag[0, u, :, :, :, pl.ds(i * BLK, BLK)].reshape(TOK, BLK).T
-            grads = full[1].reshape(TOK, FT)
+            grads = full[pl.ds(16, 16)].reshape(TOK, FT)
             value = jnp.dot(act_t[...], grads, preferred_element_type=F32).astype(BF16)
             for c in range(FB):
                 dense2[pl.ds(c * UB + u * UPI, UPI)] = value[:, c * BLK : (c + 1) * BLK].reshape(UPI, BLK, BLK)
@@ -317,38 +351,40 @@
         save.start()
         saves.append(save)
 
-    def piece(a, p, q):
-        return po.at[a, p, q] if a == 0 else po.at[a, q, p]
+    def piece(a, h, p, q):
+        return po.at[a, p, q, :, lanes[h]] if h == 0 else po.at[a, q, p, :, lanes[h]]
 
     far = ((zo, zr, zl, z), (yo, yr, yl, y))
-    mine_p = (y, z)
     peers = ((yr, yl, yo), (zr, zl, zo))
     peer_devs = (dev_y, dev_z)
     last_devs = ((dev_z[2], dev_z[0], dev_z[1]), (dev_y[2], dev_y[0], dev_y[1]))
 
     def step_c(u, a):
-        if u == 0:
-            for n in range(4):
-                flight["c1", n, a] = [
-                    send(piece(a, peers[a][d], far[a][n]), c1.at[a, n, d], peer_devs[a][d]) for d in (2, 0, 1)
-                ]
-        elif u <= 4:
-            n = u - 1
-            for copy in flight["c1", n, a]:
-                copy.wait_recv()
-            spot = piece(a, mine_p[a], far[a][n])
-            total = spot[...].astype(F32)
-            for d in range(3):
-                total = total + c1[a, n, d].astype(F32)
-            spot[...] = total.astype(BF16)
-            if n < 3:
-                flight["c2", n, a] = send(spot, c2.at[a, n], last_devs[a][n])
-        else:
-            total = piece(a, mine_p[a], far[a][3])[...].astype(F32)
-            for n in range(3):
-                flight["c2", n, a].wait_recv()
-                total = total + c2[a, n].astype(F32)
-            (out_ref, gin_ref)[a][...] = total.astype(BF16)
+        for n in range(4) if u == 0 else ():
+            for h in (0, 1):
+                flight["c1", n, a, h] = fresh()
+                for d in (2, 0, 1):
+                    there = piece(a, h, peers[h][d], far[h][n])
+                    send(there, c1.at[a, h, n, d], peer_devs[h][d], 3, flight["c1", n, a, h])
+        for h in (0, 1) if u > 0 else ():
+            if u <= 4:
+                n = u - 1
+                wait_bytes(c1.at[a, h, n], recv_sems.at[flight["c1", n, a, h]])
+                spot = piece(a, h, own[h], far[h][n])
+                total = spot[...].astype(F32)
+                for d in range(3):
+                    total = total + c1[a, h, n, d].astype(F32)
+                spot[...] = total.astype(BF16)
+                if n == 0:
+                    flight["c2", a, h] = fresh()
+                if n < 3:
+                    send(spot, c2.at[a, h, n], last_devs[h][n], 4, flight["c2", a, h])
+            else:
+                total = piece(a, h, own[h], far[h][3])[...].astype(F32)
+                wait_bytes(c2.at[a, h], recv_sems.at[flight["c2", a, h]])
+                for n in range(3):
+                    total = total + c2[a, h, n].astype(F32)
+                (out_ref, gin_ref)[a][:, lanes[h]] = total.astype(BF16)
 
     steps = {
         "F": step_f,
@@ -368,12 +404,15 @@
         for name in line.split():
             steps[name[0]](int(name[1]), "hg".index(name[2]))
 
-    for copy in started:
-        copy.wait_send()
+    wait_bytes(full.at[pl.ds(0, 30)], send_sems.at[0])
+    wait_bytes(ag, send_sems.at[1])
+    wait_bytes(ag.at[:, :, :, pl.ds(0, 3)], send_sems.at[2])
+    wait_bytes(c1, send_sems.at[3])
+    wait_bytes(c2, send_sems.at[4])
     saves[-1].wait()
 
 
-N_SEMS = 30 + 22 * ITEMS + 30
+N_SEMS = 14 + 14 * ITEMS + 20
 
 
 def fused(tokens, out_grad, idx1, idx2, w1, w2):
@@ -394,17 +433,16 @@
             pltpu.VMEM((CAP + 1, BLK, BLK), BF16),
             pltpu.VMEM((NONE + 1, BLK, BLK), BF16),
             pltpu.VMEM((NONE + 1, BLK, BLK), BF16),
-            pltpu.VMEM((2, 4, 4, 16, FT), BF16),
+            pltpu.VMEM((32, 16, FT), BF16),
             pltpu.VMEM((2, ITEMS, 2, 4, 32, NU), BF16),
             pltpu.VMEM((2, ITEMS, 32, NU), BF16),
-            pltpu.VMEM((2, ITEMS, 32, NU), BF16),
-            pltpu.VMEM((2, ITEMS, 32, NU), BF16),
+            pltpu.VMEM((2, ITEMS, 2, 32, NU), BF16),
             pltpu.VMEM((ITEMS, 32, NU), F32),
             pltpu.VMEM((2, ITEMS, 2, 4, 32, NU), BF16),
             pltpu.VMEM((2, TOK, FT), F32),
             pltpu.VMEM((2, 4, 4, 16, FT), BF16),
-            pltpu.VMEM((2, 4, 3, 16, FT), BF16),
-            pltpu.VMEM((2, 3, 16, FT), BF16),
+            pltpu.VMEM((2, 2, 4, 3, 16, FT // 2), BF16),
+            pltpu.VMEM((2, 2, 3, 16, FT // 2), BF16),
             pltpu.VMEM((FT, TOK), BF16),
             pltpu.VMEM((NU, TOK), BF16),
             pltpu.VMEM((2, 2, CAP), I32),
@@ -412,7 +450,7 @@
             pltpu.SMEM((2, CAP), I32),
             pltpu.VMEM((8, BLK), I32),
             pltpu.SMEM((8, BLK), I32),
-            pltpu.SemaphoreType.DMA((N_SEMS,)),
+            pltpu.SemaphoreType.DMA((5,)),
             pltpu.SemaphoreType.DMA((N_SEMS,)),
             pltpu.SemaphoreType.DMA((11,)),
         ],

time: 77.7 us -> 68.5 us (0.88)
  Pallas kernels: 76.8 us -> 67.6 us
    pallas_call x1, Pallas kernels: 72.2 us -> 63 us  [fused(): pl.pallas_call(fused_kernel, out_shape=(jax.ShapeDtypeStruct((16, FT), BF...]
where the time goes in v2:
time: 68.5 us; the launch traced here: 68.4 us
  Pallas kernels  67.6 us (99%)
  between operations  0.8 us (1%)
    pallas_call x1, Pallas kernels, fused(): pl.pallas_call(fused_kernel, out_shape=(jax.ShapeDtypeStruct((16, FT), BF...  63 us
    pallas_call x1, Pallas kernels, place(): pl.pallas_call(place_kernel, out_shape=(shape, shape, small, small), in_s...  4.56 us

profile of v2, /device:TPU:0, one launch (start us, length us, event | category | flops | bytes accessed | tf_op | source)
XLA Modules:
  0.0 68.4 jit_solution(7541392180918725262)
XLA Ops:
  0.6 63.0 %ffn_fused.1 = (bf16[16,1536]{1,0:T(8,128)(2,1)S(1)}, bf16[16,1536]{1,0:T(8,128)(2,1)S(1)}, bf16[180,128,128]{2,1,0:T(8,128)(2,1)S(1)}, bf16[180,128,128]{2,1,0:T(8,128)(2,1)S(1)}) custom-call(bf16[16,1536]{1,0:T(8,128)(2,1)} %tok_hbm.1, bf16[16,1536]{1,0:T(8,128)(2,1)} %grad_hbm.1, s32[2,180]{1,0:T(2,128)} %bitcast.2, s32[2,180]{1,0:T(2,128)} %bitcast.3, ...), custom_call_target="tpu_custom_call" | custom-call | flops 14495514624 | bytes 31000000 | tf_op jit(solution)/shard_map/ffn_fused/pallas_call | solution.py:422
  63.7 4.6 %ffn_place.1 = (bf16[180,128,128]{2,1,0:T(8,128)(2,1)}, bf16[180,128,128]{2,1,0:T(8,128)(2,1)}, bf16[16,1536]{1,0:T(8,128)(2,1)}, bf16[16,1536]{1,0:T(8,128)(2,1)}) custom-call(bf16[180,128,128]{2,1,0:T(8,128)(2,1)S(1)} %get-tuple-element.12.dw1, bf16[180,128,128]{2,1,0:T(8,128)(2,1)S(1)} %get-tuple-element.13.dw2, ...), custom_call_target="tpu_custom_call" | custom-call | bytes 24000000 | tf_op jit(solution)/shard_map/ffn_place/pallas_call | solution.py:480

commit v3 on v2

--- a/solution.py
+++ b/solution.py
@@ -24,14 +24,14 @@
 NT = (((1,), (1,)), ((), ()))
 
 ORDER = (
-    "F0h F1h F2h F3h", "10h 11h F4h 12h", "F5h 13h F0g 14h", "F1g 20h 15h 21h",
-    "F2g 10g 22h F3g", "11g 23h F4g 12g", "24h 30h 13g 25h", "T0h 31h 14g 20g",
-    "32h 21g 33h 22g", "F5g 50h 34h 40h", "15g 23g 35h 51h", "41h 24g 42h 30g",
-    "31g 52h 53h 43h", "44h 32g 60h 54h", "25g B0h 45h 33g", "55h 61h W0h 62h",
-    "34g B1h 40g 50g", "B2h 41g 51g 64h", "63h W1h 52g 42g", "W2h B3h 65h 35g",
-    "43g 53g B4h 44g", "54g B5h 60g 61g", "C0h 62g 45g 55g", "B0g 63g 64g B1g",
-    "B2g B3g B4g C1h", "65g W3h C2h W4h", "B5g C0g C3h C4h", "W5h S0h W0g W1g",
-    "W2g C1g W3g W4g", "C2g W5g S0g C3g", "C4g C5h C5g",
+    "F0h F1h F3h 10h", "F2h 11h F4h 13h", "F5h 12h 14h F2g", "15h F1g 20h 21h",
+    "12g F0g 11g 22h", "23h 24h 10g 31h", "25h F4g 30h 32h", "F3g 34h 14g 13g",
+    "51h T0h 40h 33h", "41h 20g F5g 42h", "21g 15g 44h 50h", "35h 22g 23g 54h",
+    "43h 60h 61h 53h", "24g B0h 30g 52h", "W0h 62h 45h 31g", "25g B1h 32g 64h",
+    "63h B2h 33g 34g", "W2h B3h 55h 65h", "40g 41g B4h 51g", "35g W3h 42g B5h",
+    "43g C0h 44g 50g", "61g 60g W5h W4h", "45g 54g 52g W1h", "53g 62g 55g B0g",
+    "63g B1g C1h 64g", "B2g 65g B3g B4g", "B5g C0g C2h S0h", "W3g W1g W5g W2g",
+    "W4g C1g W0g C3h", "S0g C2g C3g C4h", "C4g C5h C5g",
 )
 
 
@@ -225,6 +225,7 @@
     x_ahead = (xr, xl)
     x_behind = (xl, xr)
     flight = {}
+    ready = []
 
     def tile1(u, rows, count):
         return jnp.concatenate(
@@ -237,8 +238,9 @@
         )
 
     def step_f(u, a):
-        if a == 1 and u == 0:
+        if a == 1 and not ready:
             gathered(1)
+            ready.append(u)
         tokens = full[pl.ds(a * 16, 16)].reshape(TOK, FT)
         if a == 0:
             hidden = jnp.dot(tokens, tile1(u, 0, FB), preferred_element_type=F32)

time: 68.5 us -> 67.5 us (0.985)
  Pallas kernels: 67.6 us -> 66.5 us
    pallas_call x1, Pallas kernels: 63 us -> 62 us  [fused(): pl.pallas_call(fused_kernel, out_shape=(jax.ShapeDtypeStruct((16, FT), BF...]
where the time goes in v3:
time: 67.5 us; the launch traced here: 67.3 us
  Pallas kernels  66.5 us (99%)
  between operations  0.8 us (1%)
    pallas_call x1, Pallas kernels, fused(): pl.pallas_call(fused_kernel, out_shape=(jax.ShapeDtypeStruct((16, FT), BF...  62 us
    pallas_call x1, Pallas kernels, place(): pl.pallas_call(place_kernel, out_shape=(shape, shape, small, small), in_s...  4.56 us

profile of v3, /device:TPU:0, one launch (start us, length us, event | category | flops | bytes accessed | tf_op | source)
XLA Modules:
  0.0 67.3 jit_solution(1905831802593359348)
XLA Ops:
  0.6 62.0 %ffn_fused.1 = (bf16[16,1536]{1,0:T(8,128)(2,1)S(1)}, bf16[16,1536]{1,0:T(8,128)(2,1)S(1)}, bf16[180,128,128]{2,1,0:T(8,128)(2,1)S(1)}, bf16[180,128,128]{2,1,0:T(8,128)(2,1)S(1)}) custom-call(bf16[16,1536]{1,0:T(8,128)(2,1)} %tok_hbm.1, bf16[16,1536]{1,0:T(8,128)(2,1)} %grad_hbm.1, s32[2,180]{1,0:T(2,128)} %bitcast.2, s32[2,180]{1,0:T(2,128)} %bitcast.3, ...), custom_call_target="tpu_custom_call" | custom-call | flops 14495514624 | bytes 31000000 | tf_op jit(solution)/shard_map/ffn_fused/pallas_call | solution.py:424
  62.6 4.6 %ffn_place.1 = (bf16[180,128,128]{2,1,0:T(8,128)(2,1)}, bf16[180,128,128]{2,1,0:T(8,128)(2,1)}, bf16[16,1536]{1,0:T(8,128)(2,1)}, bf16[16,1536]{1,0:T(8,128)(2,1)}) custom-call(bf16[180,128,128]{2,1,0:T(8,128)(2,1)S(1)} %get-tuple-element.12.dw1, bf16[180,128,128]{2,1,0:T(8,128)(2,1)S(1)} %get-tuple-element.13.dw2, ...), custom_call_target="tpu_custom_call" | custom-call | bytes 24000000 | tf_op jit(solution)/shard_map/ffn_place/pallas_call | solution.py:482

commit v4 on v3

--- a/solution.py
+++ b/solution.py
@@ -158,7 +158,11 @@
         return [send(ref, ref, dev, 0, recv) for dev in devs]
 
     def gather_one(a):
-        return [spread_to(slot(a, h, near[h][0], own[h]), first[h]) for h in (0, 1)]
+        recvs = [fresh() for _ in range(3)]
+        for h in (0, 1):
+            for dev, recv in zip(first[h], recvs):
+                spread_to(slot(a, h, near[h][0], own[h]), (dev,), recv)
+        return recvs
 
     everything = (fresh(), fresh())
 
@@ -200,8 +204,7 @@
     places_of.start()
     def gather_rest(a):
         for step, mirror in ((1, 1), (2, 0), (3, 2)):
-            for h in (0, 1):
-                stage_a[a][h][mirror].wait_recv()
+            wait_bytes(full.at[0], recv_sems.at[stage_a[a][mirror]])
             gather_two(a, step)
 
     gather_rest(0)
@@ -247,14 +250,15 @@
         else:
             hidden = lax.dot_general(tokens, tile2(u, 0, FB), NT, preferred_element_type=F32)
         part[a, u] = hidden.astype(BF16).reshape(2, 4, 32, NU)
-        flight["core", u, a] = send(part.at[a, u, 1 - k], ag.at[a, u, 1 - k], sib, 1)
+        flight["sems", u, a] = (fresh(), fresh())
+        flight["core", u, a] = send(part.at[a, u, 1 - k], ag.at[a, u, 1 - k], sib, 1, flight["sems", u, a][0])
 
     def step_1(u, a):
         d = (u + a) % 2
         flight["core", u, a].wait_recv()
         for where in (xo, x_behind[d], x_ahead[d], x):
             part[a, u, k, where] = add(part[a, u, k, where], ag[a, u, k, where])
-        flight["m1a", u, a] = send(part.at[a, u, k, xo], m1a.at[a, u], ahead[d], 2)
+        flight["m1a", u, a] = send(part.at[a, u, k, xo], m1a.at[a, u], ahead[d], 2, flight["sems", u, a][1])
         flight["last", u, a] = fresh()
         send(part.at[a, u, k, x_behind[d]], mm.at[a, u, 0], behind[d], 2, flight["last", u, a])
 
@@ -275,8 +279,8 @@
         else:
             ag[a, u, k, x] = (total * slope[u]).astype(BF16)
         mine = ag.at[a, u, k, x]
-        flight["agd", u, a] = send(mine, mine, ahead[d], 2)
-        flight["ago", u, a] = send(mine, mine, behind[d], 2)
+        flight["agd", u, a] = send(mine, mine, ahead[d], 2, flight["sems", u, a][0])
+        flight["ago", u, a] = send(mine, mine, behind[d], 2, flight["sems", u, a][1])
 
     arrived = {}
 
@@ -363,27 +367,29 @@
 
     def step_c(u, a):
         for n in range(4) if u == 0 else ():
+            flight["c1", n, a] = fresh()
             for h in (0, 1):
-                flight["c1", n, a, h] = fresh()
                 for d in (2, 0, 1):
                     there = piece(a, h, peers[h][d], far[h][n])
-                    send(there, c1.at[a, h, n, d], peer_devs[h][d], 3, flight["c1", n, a, h])
+                    send(there, c1.at[a, n, h, d], peer_devs[h][d], 3, flight["c1", n, a])
+        if 1 <= u <= 4:
+            wait_bytes(c1.at[a, u - 1], recv_sems.at[flight["c1", u - 1, a]])
+        if u == 1:
+            flight["c2", a] = fresh()
+        if u == 5:
+            wait_bytes(c2.at[a], recv_sems.at[flight["c2", a]])
         for h in (0, 1) if u > 0 else ():
             if u <= 4:
                 n = u - 1
-                wait_bytes(c1.at[a, h, n], recv_sems.at[flight["c1", n, a, h]])
                 spot = piece(a, h, own[h], far[h][n])
                 total = spot[...].astype(F32)
                 for d in range(3):
-                    total = total + c1[a, h, n, d].astype(F32)
+                    total = total + c1[a, n, h, d].astype(F32)
                 spot[...] = total.astype(BF16)
-                if n == 0:
-                    flight["c2", a, h] = fresh()
                 if n < 3:
-                    send(spot, c2.at[a, h, n], last_devs[h][n], 4, flight["c2", a, h])
+                    send(spot, c2.at[a, h, n], last_devs[h][n], 4, flight["c2", a])
             else:
                 total = piece(a, h, own[h], far[h][3])[...].astype(F32)
-                wait_bytes(c2.at[a, h], recv_sems.at[flight["c2", a, h]])
                 for n in range(3):
                     total = total + c2[a, h, n].astype(F32)
                 (out_ref, gin_ref)[a][:, lanes[h]] = total.astype(BF16)
@@ -414,7 +420,7 @@
     saves[-1].wait()
 
 
-N_SEMS = 14 + 14 * ITEMS + 20
+N_SEMS = 8 + 10 * ITEMS + 10
 
 
 def fused(tokens, out_grad, idx1, idx2, w1, w2):
@@ -443,7 +449,7 @@
             pltpu.VMEM((2, ITEMS, 2, 4, 32, NU), BF16),
             pltpu.VMEM((2, TOK, FT), F32),
             pltpu.VMEM((2, 4, 4, 16, FT), BF16),
-            pltpu.VMEM((2, 2, 4, 3, 16, FT // 2), BF16),
+            pltpu.VMEM((2, 4, 2, 3, 16, FT // 2), BF16),
             pltpu.VMEM((2, 2, 3, 16, FT // 2), BF16),
             pltpu.VMEM((FT, TOK), BF16),
             pltpu.VMEM((NU, TOK), BF16),

time: 67.5 us -> 67.1 us (level)
  no operation moved by 1% of the time
where the time goes in v4:
time: 67.1 us; the launch traced here: 67 us
  Pallas kernels  66.2 us (99%)
  between operations  0.8 us (1%)
    pallas_call x1, Pallas kernels, fused(): pl.pallas_call(fused_kernel, out_shape=(jax.ShapeDtypeStruct((16, FT), BF...  61.6 us
    pallas_call x1, Pallas kernels, place(): pl.pallas_call(place_kernel, out_shape=(shape, shape, small, small), in_s...  4.56 us

profile of v4, /device:TPU:0, one launch (start us, length us, event | category | flops | bytes accessed | tf_op | source)
XLA Modules:
  0.0 67.0 jit_solution(8682410250560693421)
XLA Ops:
  0.6 61.6 %ffn_fused.1 = (bf16[16,1536]{1,0:T(8,128)(2,1)S(1)}, bf16[16,1536]{1,0:T(8,128)(2,1)S(1)}, bf16[180,128,128]{2,1,0:T(8,128)(2,1)S(1)}, bf16[180,128,128]{2,1,0:T(8,128)(2,1)S(1)}) custom-call(bf16[16,1536]{1,0:T(8,128)(2,1)} %tok_hbm.1, bf16[16,1536]{1,0:T(8,128)(2,1)} %grad_hbm.1, s32[2,180]{1,0:T(2,128)} %bitcast.2, s32[2,180]{1,0:T(2,128)} %bitcast.3, ...), custom_call_target="tpu_custom_call" | custom-call | flops 14495514624 | bytes 31000000 | tf_op jit(solution)/shard_map/ffn_fused/pallas_call | solution.py:430
  62.3 4.6 %ffn_place.1 = (bf16[180,128,128]{2,1,0:T(8,128)(2,1)}, bf16[180,128,128]{2,1,0:T(8,128)(2,1)}, bf16[16,1536]{1,0:T(8,128)(2,1)}, bf16[16,1536]{1,0:T(8,128)(2,1)}) custom-call(bf16[180,128,128]{2,1,0:T(8,128)(2,1)S(1)} %get-tuple-element.12.dw1, bf16[180,128,128]{2,1,0:T(8,128)(2,1)S(1)} %get-tuple-element.13.dw2, ...), custom_call_target="tpu_custom_call" | custom-call | bytes 24000000 | tf_op jit(solution)/shard_map/ffn_place/pallas_call | solution.py:488
